TPU v7x, 32 devices: a whole 2x2x4 slice. The times are simulated.
32 devices in a mesh: src: 4 (over y, x), dst: 8 (over z, core).
Axes of the slice: x: 2, y: 2, z: 4, core: 2. Of those that a mesh axis runs over, the one named last changes fastest.
Arguments:
- density0: float32 [16, 16384], P(None, ('src', 'dst')), may hold values from 0.2 to 5
- logits: float32 [2, 16, 16384], P(None, None, ('src', 'dst')), may hold values from -6 to 6
- value_final: float32 [16, 16384], P(None, ('src', 'dst')), may hold values from -6 to 6
- base_reward: float32 [2, 16, 16384], P(None, None, ('src', 'dst')), may hold values from -6 to 6
- crowd: float32 [16], replicated, may hold values from 0.2 to 2
- tiles: bfloat16 [4, 8, 2, 8, 256, 256], P('src', 'dst'), may hold values from 0 to 0.75
- tile_src: int32 [4, 8, 2, 8], P('src', 'dst'), may hold values from 0 to 15
- tile_dst: int32 [4, 8, 2, 8], P('src', 'dst'), may hold values from 0 to 7
- tile_count: int32 [4, 8, 2], P('src', 'dst'), may hold values from 2 to 8, as said below
Outputs:
- new_logits: float32 [2, 16, 16384], P(None, None, ('src', 'dst'))
- value_start: float32 [16, 16384], P(None, ('src', 'dst'))
- density_final: float32 [16, 16384], P(None, ('src', 'dst'))
Inputs may be any that keep to these rules, and one draw needn't show every extreme that they name: `tile_count`: slots at or past the count are ignored. In every draw some device holds 8 live slots for some action.
All inputs are finite; a program needn't handle non-finite values.
Results may differ from a plain program's by a relative error of at most 0.0011.
Values may be sent and summed in bfloat16 or wider, within the bound.
A program may use at most 64 MiB of HBM per device.

v0:
```python
import jax
import jax.numpy as jnp
from jax import lax
from jax.sharding import PartitionSpec as P

P_SIZE = 16
A = 2
B = 256
BPZ = 2
TCAP = 8
H = 4


discount = 0.9
step_size = 1.0


def policy_of(logits):
    margin = logits[0] - logits[1]
    return jnp.stack([jax.nn.sigmoid(margin), jax.nn.sigmoid(-margin)])


def reward_of(base_reward, crowd, density):
    crowding = jnp.log1p(jnp.mean(density, axis=0))
    return base_reward - crowd[None, :, None] * crowding[None, None, :]


def take_rows(block_set, row_index):
    return jnp.take(block_set, row_index, axis=1)


def body(density0, logits, value_final, base_reward, crowd, tiles, tile_src, tile_dst, tile_count):
    src_count = lax.axis_size("src")
    dst_count = lax.axis_size("dst")
    tile_block = tiles[0, 0]
    src_rows = tile_src[0, 0]
    dst_rows = tile_dst[0, 0]
    filled = tile_count[0, 0]
    shard_states = density0.shape[1]
    src_blocks = BPZ * dst_count
    dst_blocks = BPZ * src_count
    all_states = shard_states * src_count * dst_count
    slot_live = (jnp.arange(TCAP, dtype=jnp.int32)[None, :] < filled[:, None]).astype(jnp.float32)
    to_dst = jax.nn.one_hot(dst_rows, dst_blocks, dtype=jnp.float32) * slot_live[:, :, None]
    to_src = jax.nn.one_hot(src_rows, src_blocks, dtype=jnp.float32) * slot_live[:, :, None]
    policy_now = policy_of(logits)
    densities = [density0]
    for moment in range(H):
        weighted = (policy_now * densities[-1][None]).astype(jnp.bfloat16)
        gathered = lax.all_gather(weighted, "dst", axis=2, tiled=True)
        blocks = gathered.reshape(A, P_SIZE, src_blocks, B)
        advance_picked = jax.vmap(take_rows)(blocks, src_rows)
        advance_product = jnp.einsum(
            "apki,akij->apkj", advance_picked, tile_block, preferred_element_type=jnp.float32
        )
        arrived = jnp.einsum(
            "akc,apkj->pcj", to_dst, advance_product, precision=lax.Precision.HIGHEST
        ).reshape(P_SIZE, dst_blocks * B)
        population_mass = lax.psum(jnp.sum(arrived, axis=1), ("src", "dst"))
        shared = lax.psum_scatter(arrived, "src", scatter_dimension=1, tiled=True)
        densities.append(shared * (all_states / population_mass)[:, None])
    value_next = value_final
    action_value = base_reward
    for moment in reversed(range(H)):
        value_half = value_next.astype(jnp.bfloat16)
        value_group = lax.all_gather(value_half, "src", axis=1, tiled=True).reshape(
            P_SIZE, dst_blocks, B
        )
        picked = jnp.take(value_group, dst_rows, axis=1)
        product = jnp.einsum(
            "akij,pakj->apki", tile_block, picked, preferred_element_type=jnp.float32
        )
        returned = jnp.einsum(
            "aks,apki->apsi", to_src, product, precision=lax.Precision.HIGHEST
        ).reshape(A, P_SIZE, src_blocks * B)
        summed = lax.psum_scatter(returned, "dst", scatter_dimension=2, tiled=True)
        evaluate_action_value = reward_of(base_reward, crowd, densities[moment]) + discount * summed
        value_next = jnp.sum(policy_now * evaluate_action_value, axis=0)
        action_value = evaluate_action_value
    new_logits = logits + step_size * action_value
    return (new_logits, value_next, densities[-1])


def solution(mesh):
    in_specs = (
        P(None, ("src", "dst")),
        P(None, None, ("src", "dst")),
        P(None, ("src", "dst")),
        P(None, None, ("src", "dst")),
        P(),
        P("src", "dst", None, None, None, None),
        P("src", "dst", None, None),
        P("src", "dst", None, None),
        P("src", "dst", None),
    )
    out_specs = (P(None, None, ("src", "dst")), P(None, ("src", "dst")), P(None, ("src", "dst")))
    return jax.shard_map(body, mesh=mesh, in_specs=in_specs, out_specs=out_specs, check_vma=False)
```

profile of v0, /device:TPU:0, one launch (start us, length us, event | category | flops | bytes accessed | tf_op | source)
XLA Modules:
  0.0 357.4 jit_solution(13770647321593170806)
XLA Ops:
  7.2 0.8 bitcast_or_fusion
  8.1 0.7 compare_and_fusion.1
  8.7 0.7 compare_convert_fusion
  9.5 0.8 add_divide_fusion.1
  10.3 0.8 multiply_convert_fusion.3
  11.0 15.9 %all_gather.24 = bf16[2,16,4096]{2,1,0:T(8,128)(2,1)S(1)} all-gather(bf16[2,16,512]{2,1,0:T(8,128)(2,1)S(1)} %multiply_convert_fusion.3), channel_id=1, replica_groups=mesh['src'=4,'dst'=8] {'dst'}, dimensions={2}, use_global_device_ids=true | all-gather | bytes 294912 | tf_op jit(solution)/shard_map/all_gather | solution.py:50
  26.9 0.1 reshape.330
  27.0 0.6 gather_fusion
  27.6 0.4 fusion.16
  28.0 0.6 bitcast_reduce_fusion.3
  28.6 0.7 copy.41
  29.4 40.3 %psum.28 = f32[16]{0:T(128)S(1)} all-reduce(f32[16]{0:T(128)S(1)} %get-tuple-element.21), channel_id=1, replica_groups=mesh['src'=4,'dst'=8] {'src','dst'}, use_global_device_ids=true, to_apply=%region_3.5 | all-reduce | flops 16 | bytes 128 | tf_op jit(solution)/shard_map/psum | solution.py:59
  69.7 0.1 reshape.344
  69.8 0.8 fusion.141
  70.7 14.3 %all_gather.25 = bf16[2,16,4096]{2,1,0:T(8,128)(2,1)S(1)} all-gather(bf16[2,16,512]{2,1,0:T(8,128)(2,1)S(1)} %multiply_convert_fusion.2), channel_id=1, replica_groups=mesh['src'=4,'dst'=8] {'dst'}, dimensions={2}, use_global_device_ids=true | all-gather | bytes 294912 | tf_op jit(solution)/shard_map/all_gather | solution.py:50
  85.0 0.6 gather_fusion.1
  85.6 0.4 fusion.19
  86.0 0.6 bitcast_reduce_fusion.2
  86.6 0.7 copy.42
  87.4 9.0 %all_gather.27 = bf16[16,2048]{1,0:T(8,128)(2,1)S(1)} all-gather(bf16[16,512]{1,0:T(8,128)(2,1)S(1)} %convert_element_type.39), channel_id=1, replica_groups=mesh['src'=4,'dst'=8] {'src'}, dimensions={1}, use_global_device_ids=true | all-gather | bytes 81920 | tf_op jit(solution)/shard_map/all_gather | solution.py:66
  96.4 0.6 gather_fusion.3
  97.0 37.5 %psum.29 = f32[16]{0:T(128)S(1)} all-reduce(f32[16]{0:T(128)S(1)} %get-tuple-element.23), channel_id=1, replica_groups=mesh['src'=4,'dst'=8] {'src','dst'}, use_global_device_ids=true, to_apply=%region_7.9 | all-reduce | flops 16 | bytes 128 | tf_op jit(solution)/shard_map/psum | solution.py:59
  134.5 0.9 fusion.142
  135.4 14.3 %all_gather.26 = bf16[2,16,4096]{2,1,0:T(8,128)(2,1)S(1)} all-gather(bf16[2,16,512]{2,1,0:T(8,128)(2,1)S(1)} %multiply_convert_fusion.1), channel_id=1, replica_groups=mesh['src'=4,'dst'=8] {'dst'}, dimensions={2}, use_global_device_ids=true | all-gather | bytes 294912 | tf_op jit(solution)/shard_map/all_gather | solution.py:50
  149.7 0.6 gather_fusion.2
  150.3 0.4 fusion.22
  150.7 0.6 bitcast_reduce_fusion.1
  151.3 0.7 copy.43
  152.1 0.7 fusion.25
  152.8 0.8 convolution_bitcast_fusion.3
  153.6 0.9 reshape.236
  154.6 39.1 %psum.30 = f32[16]{0:T(128)S(1)} all-reduce(f32[16]{0:T(128)S(1)} %get-tuple-element.25), channel_id=1, replica_groups=mesh['src'=4,'dst'=8] {'src','dst'}, use_global_device_ids=true, to_apply=%region_11.13 | all-reduce | flops 16 | bytes 128 | tf_op jit(solution)/shard_map/psum | solution.py:59
  193.7 0.8 fusion.143
  194.5 0.1 broadcast_multiply_fusion.7
  194.6 14.4 %reduce-scatter.15.cloned.1.call-done = f32[2,16,512]{2,1,0:T(8,128)} async-done(((f32[2,16,4096]{2,1,0:T(8,128)}), f32[2,16,512]{2,1,0:T(8,128)}) %reduce-scatter.15.cloned.1.call-update) | async-done | bytes 65552 | tf_op jit(solution)/shard_map/reduce_scatter | solution.py:76
  209.0 0.9 multiply_convert_fusion
  209.9 8.3 %all_gather.28 = bf16[16,2048]{1,0:T(8,128)(2,1)S(1)} all-gather(bf16[16,512]{1,0:T(8,128)(2,1)S(1)} %get-tuple-element.14), channel_id=1, replica_groups=mesh['src'=4,'dst'=8] {'src'}, dimensions={1}, use_global_device_ids=true | all-gather | bytes 81920 | tf_op jit(solution)/shard_map/all_gather | solution.py:66
  218.2 0.6 gather_fusion.4
  218.7 0.7 fusion.28
  219.4 0.8 convolution_bitcast_fusion.2
  220.2 0.9 reshape.238
  221.1 28.3 %reduce-scatter.17.cloned.1.call-done = f32[2,16,512]{2,1,0:T(8,128)} async-done(((f32[2,16,4096]{2,1,0:T(8,128)}), f32[2,16,512]{2,1,0:T(8,128)}) %reduce-scatter.17.cloned.1.call-update) | async-done | bytes 65552 | tf_op jit(solution)/shard_map/reduce_scatter | solution.py:76
  249.4 0.9 multiply_reduce_fusion.2
  250.2 8.5 %all_gather.29 = bf16[16,2048]{1,0:T(8,128)(2,1)S(1)} all-gather(bf16[16,512]{1,0:T(8,128)(2,1)S(1)} %multiply_reduce_fusion.2), channel_id=1, replica_groups=mesh['src'=4,'dst'=8] {'src'}, dimensions={1}, use_global_device_ids=true | all-gather | bytes 81920 | tf_op jit(solution)/shard_map/all_gather | solution.py:66
  258.7 0.6 gather_fusion.5
  259.3 0.7 fusion.31
  259.9 0.8 convolution_bitcast_fusion.1
  260.7 0.9 reshape.240
  261.7 14.4 %all_gather.31 = bf16[2,16,4096]{2,1,0:T(8,128)(2,1)S(1)} all-gather(bf16[2,16,512]{2,1,0:T(8,128)(2,1)S(1)} %get-tuple-element.13), channel_id=1, replica_groups=mesh['src'=4,'dst'=8] {'dst'}, dimensions={2}, use_global_device_ids=true | all-gather | bytes 294912 | tf_op jit(solution)/shard_map/all_gather | solution.py:50
  276.1 0.6 gather_fusion.7
  276.6 0.4 fusion.37
  277.1 0.6 bitcast_reduce_fusion
  277.7 0.7 copy.44
  278.4 11.8 %reduce-scatter.19.cloned.1.call-done = f32[2,16,512]{2,1,0:T(8,128)} async-done(((f32[2,16,4096]{2,1,0:T(8,128)}), f32[2,16,512]{2,1,0:T(8,128)}) %reduce-scatter.19.cloned.1.call-update) | async-done | bytes 65552 | tf_op jit(solution)/shard_map/reduce_scatter | solution.py:76
  290.2 0.9 multiply_reduce_fusion.1
  291.1 8.2 %all_gather.30 = bf16[16,2048]{1,0:T(8,128)(2,1)S(1)} all-gather(bf16[16,512]{1,0:T(8,128)(2,1)S(1)} %multiply_reduce_fusion.1), channel_id=1, replica_groups=mesh['src'=4,'dst'=8] {'src'}, dimensions={1}, use_global_device_ids=true | all-gather | bytes 81920 | tf_op jit(solution)/shard_map/all_gather | solution.py:66
  299.3 0.6 gather_fusion.6
  299.9 0.7 fusion.34
  300.6 0.8 convolution_bitcast_fusion
  301.3 0.9 reshape.242
  302.2 37.0 %psum.31 = f32[16]{0:T(128)S(1)} all-reduce(f32[16]{0:T(128)S(1)} %get-tuple-element.27), channel_id=1, replica_groups=mesh['src'=4,'dst'=8] {'src','dst'}, use_global_device_ids=true, to_apply=%region_23.26 | all-reduce | flops 16 | bytes 128 | tf_op jit(solution)/shard_map/psum | solution.py:59
  339.2 1.4 broadcast_multiply_fusion
  340.7 7.8 %reduce-scatter.21.cloned.1.call-done = f32[2,16,512]{2,1,0:T(8,128)} async-done(((f32[2,16,4096]{2,1,0:T(8,128)}), f32[2,16,512]{2,1,0:T(8,128)}) %reduce-scatter.21.cloned.1.call-update) | async-done | bytes 65552 | tf_op jit(solution)/shard_map/reduce_scatter | solution.py:76
  348.4 2.1 multiply_reduce_fusion
  (59 shorter events, 0.8 us)
Async XLA Ops:
  7.2 20.4 %copy-start = (bf16[1,1,2,8,256,256]{5,4,3,2,1,0:T(8,128)(2,1)S(1)}, bf16[1,1,2,8,256,256]{5,4,3,2,1,0:T(8,128)(2,1)}, u32[]{:S(2)}) copy-start(bf16[1,1,2,8,256,256]{5,4,3,2,1,0:T(8,128)(2,1)} %param.18) | copy-start | bytes 6291460
  7.2 20.9 %copy-start.5 = (s32[1,1,2,8]{3,2,1,0:T(2,128)S(1)}, s32[1,1,2,8]{3,2,1,0:T(2,128)}, u32[]{:S(2)}) copy-start(s32[1,1,2,8]{3,2,1,0:T(2,128)} %param.20) | copy-start | bytes 196
  7.2 62.6 %reduce-scatter.9.cloned.1.call-start = ((), (), s32[]{:S(2)}) async-start(), calls=%async_computation.8 | async-start | bytes 163840 | tf_op jit(solution)/shard_map/reduce_scatter | solution.py:60
  29.4 105.2 %reduce-scatter.11.cloned.1.call-start = ((), (), s32[]{:S(2)}) async-start(), calls=%async_computation.9 | async-start | bytes 163840 | tf_op jit(solution)/shard_map/reduce_scatter | solution.py:60
  85.0 2.4 copy-start.4
  87.3 106.4 %reduce-scatter.13.cloned.1.call-start = ((), (), s32[]{:S(2)}) async-start(), calls=%async_computation.10 | async-start | bytes 163840 | tf_op jit(solution)/shard_map/reduce_scatter | solution.py:60
  150.7 2.1 copy-start.6
  152.1 57.0 %reduce-scatter.15.cloned.1.call-start = ((), (), s32[]{:S(2)}) async-start(), calls=%async_computation.11 | async-start | bytes 589824 | tf_op jit(solution)/shard_map/reduce_scatter | solution.py:76
  152.1 2.4 copy-start.3
  152.1 42.4 %copy-start.7 = (f32[16]{0:T(128)S(1)}, f32[16]{0:T(128)}, u32[]{:S(2)}) copy-start(f32[16]{0:T(128)} %param.17) | copy-start | bytes 196
  152.1 56.9 %copy-start.1 = (f32[2,16,512]{2,1,0:T(8,128)S(1)}, f32[2,16,512]{2,1,0:T(8,128)}, u32[]{:S(2)}) copy-start(f32[2,16,512]{2,1,0:T(8,128)} %param.16) | copy-start | bytes 196612
  154.5 94.9 %reduce-scatter.17.cloned.1.call-start = ((), (), s32[]{:S(2)}) async-start(), calls=%async_computation.12 | async-start | bytes 589824 | tf_op jit(solution)/shard_map/reduce_scatter | solution.py:76
  221.1 69.2 %reduce-scatter.19.cloned.1.call-start = ((), (), s32[]{:S(2)}) async-start(), calls=%async_computation.13 | async-start | bytes 589824 | tf_op jit(solution)/shard_map/reduce_scatter | solution.py:76
  261.6 77.6 %reduce-scatter.23.cloned.1.call-start = ((), (), s32[]{:S(2)}) async-start(), calls=%async_computation.15 | async-start | bytes 163840 | tf_op jit(solution)/shard_map/reduce_scatter | solution.py:60
  278.4 70.0 %reduce-scatter.21.cloned.1.call-start = ((), (), s32[]{:S(2)}) async-start(), calls=%async_computation.14 | async-start | bytes 589824 | tf_op jit(solution)/shard_map/reduce_scatter | solution.py:76
  299.9 48.5 %copy-start.2 = (f32[2,16,512]{2,1,0:T(8,128)S(1)}, f32[2,16,512]{2,1,0:T(8,128)}, u32[]{:S(2)}) copy-start(f32[2,16,512]{2,1,0:T(8,128)} %param.14) | copy-start | bytes 196612
Sparse Core Ops, SparseCore 0:
  29.5 24.8 reduce-scatter.8
  87.4 22.9 reduce-scatter.10
  152.2 23.6 reduce-scatter.12
  178.0 30.9 reduce-scatter.14
  221.2 28.1 reduce-scatter.16
  261.7 28.4 reduce-scatter.18
  293.0 22.0 reduce-scatter.22
  317.4 30.9 reduce-scatter.20
where the time goes:
time: 358 us; the launch traced here: 357 us
  blocking collectives  247 us (69%)
  waiting for transfers between devices  62.4 us (17%)
  between operations  14.4 us (4%)
  other arithmetic  12.7 us (4%)
  local copies, waits for them, and re-layouts  11.2 us (3%)
  matrix products  9.69 us (3%)
    psum x4, blocking collectives, body(): population_mass = lax.psum(jnp.sum(arrived, axis=1), ('src', 'dst'))  154 us
    reduce_scatter x4, waiting for transfers between devices, body(): summed = lax.psum_scatter(returned, 'dst', scatter_dimension=2, tiled=True)  62.2 us
    all_gather x4, blocking collectives, body(): gathered = lax.all_gather(weighted, 'dst', axis=2, tiled=True)  58.8 us
    all_gather x4, blocking collectives, body(): lax.all_gather(value_half, 'src', axis=1, tiled=True)  34 us
  transfers between devices with their start and end apart: 8, of which 4 were waited for; matrix products, arithmetic and copies ran while one was open for 3% of the time, Pallas kernels for 0%

commit v1 on v0

v1 whole, which is shorter than its diff:
```python
import functools

import jax
import jax.numpy as jnp
from jax import lax
from jax.experimental import pallas as pl
from jax.experimental.pallas import tpu as pltpu
from jax.sharding import PartitionSpec as P

H = 4
LANES = 128
DISCOUNT = 0.9
STEP_SIZE = 1.0
MESH = pl.DeviceIdType.MESH
F32 = jnp.float32
BF16 = jnp.bfloat16


def kernel(
    S, D, N, B, BPZ, A, K,
    density0, logits, value_final, base_reward, crowd, tiles_hbm, tile_src, tile_dst, tile_count,
    new_logits, value_start, density_final,
    tiles, wbuf, pol, margin, lhs, mask, prod,
    rs_send, rs_recv, ag_send, ag_recv, ag3_send, ag3_recv, ms_send, ms_recv,
    vb0, vb1, vb2, vb3, w0buf, vr_send, vr_recv, vz_send, vz_recv, own,
    tile_sem, rs_ss, rs_rs, ag_ss, ag_rs, w0_ss, w0_rs, mg_ss, mg_rs, ms_ss, ms_rs,
    va_ss, va_rs, vr_ss, vr_rs,
):
    vbuf = (vb0, vb1, vb2, vb3)
    s = lax.axis_index("src")
    d = lax.axis_index("dst")
    PN = density0.shape[0]
    W = BPZ * B
    SB, DB = BPZ * D, BPZ * S
    src_peers = [lax.rem(s + r, S) for r in range(S)]
    dst_peers = [lax.rem(d + r, D) for r in range(D)]
    src_back = [lax.rem(s + S - r, S) for r in range(S)]
    dst_back = [lax.rem(d + D - r, D) for r in range(D)]

    def to_src(src, dst, ss, rs, r):
        return pltpu.make_async_remote_copy(
            src_ref=src, dst_ref=dst, send_sem=ss, recv_sem=rs,
            device_id=(src_peers[r], d), device_id_type=MESH)

    def to_dst(src, dst, ss, rs, r):
        return pltpu.make_async_remote_copy(
            src_ref=src, dst_ref=dst, send_sem=ss, recv_sem=rs,
            device_id=(s, dst_peers[r]), device_id_type=MESH)

    tile_copy = pltpu.make_async_copy(tiles_hbm, tiles, tile_sem)
    tile_copy.start()
    barrier = pltpu.get_barrier_semaphore()
    for r in range(1, S):
        pl.semaphore_signal(barrier, inc=1, device_id=(src_peers[r], d), device_id_type=MESH)
    for r in range(1, D):
        pl.semaphore_signal(barrier, inc=1, device_id=(s, dst_peers[r]), device_id_type=MESH)

    gap = logits[0] - logits[1]
    p0, p1 = jax.nn.sigmoid(gap), jax.nn.sigmoid(-gap)
    rho = density0[...]
    vf = value_final[...].astype(BF16)
    for b in range(BPZ):
        cols = slice(b * B, (b + 1) * B)
        w0buf[0, BPZ * d + b] = (p0 * rho)[:, cols].astype(BF16)
        w0buf[1, BPZ * d + b] = (p1 * rho)[:, cols].astype(BF16)
        margin[BPZ * d + b] = gap[:, cols]
        vbuf[3][BPZ * s + b] = vf[:, cols]
    pl.semaphore_wait(barrier, S + D - 2)

    pending = []

    def start(copy):
        copy.start()
        pending.append(copy)
        return copy

    mine = pl.ds(BPZ * d, BPZ)
    w0 = [start(to_dst(w0buf.at[:, mine], w0buf.at[:, mine], w0_ss.at[r - 1], w0_rs.at[r - 1], r)) for r in range(1, D)]

    def send_value(t):
        at = vbuf[t].at[pl.ds(BPZ * s, BPZ)]
        return [start(to_src(at, at, va_ss.at[t, r - 1], va_rs.at[t, r - 1], r)) for r in range(1, S)]

    va = {3: send_value(3)}
    mg = [start(to_dst(margin.at[mine], margin.at[mine], mg_ss.at[r - 1], mg_rs.at[r - 1], r)) for r in range(1, D)]

    for a in range(A):
        for k in range(K):
            live = jnp.where(k < tile_count[0, 0, a], 1.0, 0.0).astype(F32)
            for c in range(DB):
                hit = jnp.where(tile_dst[0, 0, a, k] == c, live, 0.0)
                mask[(a * K + k) * DB + c] = jnp.full((PN, LANES), hit, F32).astype(BF16)
    row = lax.broadcasted_iota(jnp.int32, (PN, W), 0)
    crowd_col = jnp.zeros((PN, W), F32)
    for p in range(PN):
        crowd_col = jnp.where(row == p, crowd[p], crowd_col)
    own[4] = crowd_col
    own[5] = p0
    own[6] = p1
    lane = lax.broadcasted_iota(jnp.int32, (PN, LANES), 1)

    def push(t):
        for a in range(A):
            for k in range(K):
                w = (w0buf if t == 0 else wbuf)[a, tile_src[0, 0, a, k]]
                q = a * K + k
                for c in range(DB):
                    m = mask[q * DB + c]
                    lhs[c * PN:(c + 1) * PN, q * B:(q + 1) * B] = w * jnp.concatenate([m] * (B // LANES), axis=1)
        arrived = jnp.dot(lhs[...], tiles[...], preferred_element_type=F32)
        total = arrived[0:PN]
        for c in range(1, DB):
            total = total + arrived[c * PN:(c + 1) * PN]
        lanes = sum(total[:, i:i + LANES] for i in range(0, B, LANES))
        for c in range(DB):
            rs_send[t, c // BPZ, :, (c % BPZ) * B:(c % BPZ + 1) * B] = arrived[c * PN:(c + 1) * PN]
        for c in range(S):
            rs_send[t, c, :, W:W + LANES] = lanes
        return [start(to_src(rs_send.at[t, src_peers[r]], rs_recv.at[t, r - 1], rs_ss.at[t, r - 1], rs_rs.at[t, r - 1], r))
                for r in range(1, S)]

    def owned(t, copies):
        total = rs_send[t, s]
        for r in range(1, S):
            copies[r - 1].wait_recv()
            total = total + rs_recv[t, r - 1]
        mass = jnp.sum(total[:, W:W + LANES], axis=1, keepdims=True)
        mass = jnp.broadcast_to(mass, (PN, LANES))
        hi = mass.astype(BF16).astype(F32)
        mid = (mass - hi).astype(BF16).astype(F32)
        low = mass - hi - mid
        packed = jnp.where(lane == 0, hi, jnp.where(lane == 1, mid, jnp.where(lane == 2, low, 0.0)))
        return total[:, :W], packed

    def scale_of(packed):
        mass = jnp.sum(packed, axis=1, keepdims=True)
        return N / mass

    def weigh(block, raw, scale):
        now = raw * scale
        wbuf[0, block] = (pol[0, block] * now).astype(BF16)
        wbuf[1, block] = (pol[1, block] * now).astype(BF16)

    def send_density(t, raw, packed):
        ag_send[t, :, :W] = raw.astype(BF16)
        ag_send[t, :, W:W + LANES] = packed.astype(BF16)
        return [start(to_dst(ag_send.at[t], ag_recv.at[t, r - 1], ag_ss.at[t, r - 1], ag_rs.at[t, r - 1], r))
                for r in range(1, D)]

    def take_density(t, raw, packed, copies):
        for r in range(1, D):
            copies[r - 1].wait_recv()
            packed = packed + ag_recv[t, r - 1, :, W:W + LANES].astype(F32)
        scale = scale_of(packed)
        for b in range(BPZ):
            weigh(BPZ * d + b, raw[:, b * B:(b + 1) * B], scale)
        for r in range(1, D):
            for b in range(BPZ):
                weigh(BPZ * dst_back[r] + b, ag_recv[t, r - 1, :, b * B:(b + 1) * B].astype(F32), scale)
        return raw * scale

    def send_mass(i, packed):
        ms_send[i] = packed.astype(BF16)
        return [start(to_dst(ms_send.at[i], ms_recv.at[i, r - 1], ms_ss.at[i, r - 1], ms_rs.at[i, r - 1], r))
                for r in range(1, D)]

    def take_mass(i, packed, copies):
        for r in range(1, D):
            copies[r - 1].wait_recv()
            packed = packed + ms_recv[i, r - 1].astype(F32)
        return scale_of(packed)

    def pull(t):
        for a in range(A):
            for k in range(K):
                q = a * K + k
                v = vbuf[t][tile_dst[0, 0, a, k]]
                live = jnp.where(k < tile_count[0, 0, a], 1.0, 0.0).astype(F32)
                prod[q] = live * lax.dot_general(
                    v, tiles[q * B:(q + 1) * B, :], (((1,), (1,)), ((), ())), preferred_element_type=F32)

    def collect(a, block):
        out = None
        for k in range(K):
            term = jnp.where(tile_src[0, 0, a, k] == block, 1.0, 0.0).astype(F32) * prod[a * K + k]
            out = term if out is None else out + term
        return out

    def wait_value(t):
        for copy in va[t]:
            copy.wait_recv()

    def spread(t):
        pull(t)

        def step(g, _):
            for b in range(BPZ):
                c = g * BPZ + b
                vr_send[t - 1, c] = (pol[0, c] * collect(0, c) + pol[1, c] * collect(1, c)).astype(BF16)
            return _

        lax.fori_loop(0, D, step, 0)
        return [start(to_dst(vr_send.at[t - 1, pl.ds(BPZ * dst_peers[r], BPZ)], vr_recv.at[t - 1, r - 1],
                             vr_ss.at[t, r - 1], vr_rs.at[t, r - 1], r)) for r in range(1, D)]

    def crowding(t, now):
        own[t] = own[4] * jnp.log(1.0 + jnp.mean(now, axis=0, keepdims=True))

    def gather_value(t, copies):
        for copy in copies:
            copy.wait_recv()
        for b in range(BPZ):
            cols = slice(b * B, (b + 1) * B)
            total = vr_send[t - 1, BPZ * d + b].astype(F32)
            for r in range(1, D):
                total = total + vr_recv[t - 1, r - 1, b].astype(F32)
            q0, q1 = own[5, :, cols], own[6, :, cols]
            reward = q0 * base_reward[0, :, cols] + q1 * base_reward[1, :, cols] - (q0 + q1) * own[t, :, cols]
            vbuf[t - 1][BPZ * s + b] = (reward + DISCOUNT * total).astype(BF16)
        va[t - 1] = send_value(t - 1)

    tile_copy.wait()
    for copy in w0:
        copy.wait_recv()
    rs = push(0)
    crowding(0, rho)
    for copy in mg:
        copy.wait_recv()

    def policy(c, _):
        pol[0, c] = jax.nn.sigmoid(margin[c])
        pol[1, c] = jax.nn.sigmoid(-margin[c])
        return _

    lax.fori_loop(0, SB, policy, 0)
    raw, packed = owned(0, rs)
    ag = send_density(0, raw, packed)
    now = take_density(0, raw, packed, ag)
    rs = push(1)
    crowding(1, now)
    wait_value(3)
    vr = spread(3)
    raw, packed = owned(1, rs)
    ag = send_density(1, raw, packed)
    now = take_density(1, raw, packed, ag)
    rs = push(2)
    crowding(2, now)
    raw, packed = owned(2, rs)
    ms = send_mass(0, packed)
    ag3_send[...] = raw
    scale3 = take_mass(0, packed, ms)
    now = raw * scale3
    crowding(3, now)
    gather_value(3, vr)
    ag = [start(to_dst(ag3_send, ag3_recv.at[r - 1], ag_ss.at[2, r - 1], ag_rs.at[2, r - 1], r)) for r in range(1, D)]
    wait_value(2)
    vr = spread(2)
    for copy in ag:
        copy.wait_recv()
    for b in range(BPZ):
        weigh(BPZ * d + b, raw[:, b * B:(b + 1) * B], scale3)
        for r in range(1, D):
            weigh(BPZ * dst_back[r] + b, ag3_recv[r - 1, :, b * B:(b + 1) * B], scale3)
    gather_value(2, vr)
    rs = push(3)
    wait_value(1)
    vr = spread(1)
    raw, packed = owned(3, rs)
    ms = send_mass(1, packed)
    gather_value(1, vr)
    density_final[...] = raw * take_mass(1, packed, ms)
    wait_value(0)
    pull(0)

    def both(g, _):
        for b in range(BPZ):
            c = g * BPZ + b
            for a in range(A):
                vz_send[a, c] = collect(a, c)
        return _

    lax.fori_loop(0, D, both, 0)
    vr = [start(to_dst(vz_send.at[:, pl.ds(BPZ * dst_peers[r], BPZ)], vz_recv.at[r - 1],
                       vr_ss.at[0, r - 1], vr_rs.at[0, r - 1], r)) for r in range(1, D)]
    for copy in vr:
        copy.wait_recv()
    for b in range(BPZ):
        cols = slice(b * B, (b + 1) * B)
        value = None
        for a in range(A):
            total = vz_send[a, BPZ * d + b]
            for r in range(1, D):
                total = total + vz_recv[r - 1, a, b]
            action_value = base_reward[a, :, cols] - own[0, :, cols] + DISCOUNT * total
            new_logits[a, :, cols] = logits[a, :, cols] + STEP_SIZE * action_value
            term = own[5 + a, :, cols] * action_value
            value = term if value is None else value + term
        value_start[:, cols] = value
    for copy in pending:
        copy.wait_send()


def body(density0, logits, value_final, base_reward, crowd, tiles, tile_src, tile_dst, tile_count):
    S, D = lax.axis_size("src"), lax.axis_size("dst")
    PN, W = density0.shape
    A, K, B = tiles.shape[2], tiles.shape[3], tiles.shape[-1]
    BPZ = W // B
    SB, DB = BPZ * D, BPZ * S
    N = float(W * S * D)
    vmem, smem = pl.BlockSpec(memory_space=pltpu.VMEM), pl.BlockSpec(memory_space=pltpu.SMEM)
    dma = pltpu.SemaphoreType.DMA
    V = pltpu.VMEM
    scratch = [
        V((A * K * B, B), BF16), V((A, SB, PN, B), BF16), V((A, SB, PN, B), F32), V((SB, PN, B), F32),
        V((DB * PN, A * K * B), BF16), V((A * K * DB, PN, LANES), BF16), V((A * K, PN, B), F32),
        V((H, S, PN, W + LANES), F32), V((H, S - 1, PN, W + LANES), F32),
        V((2, PN, W + LANES), BF16), V((2, D - 1, PN, W + LANES), BF16),
        V((PN, W), F32), V((D - 1, PN, W), F32), V((2, PN, LANES), BF16), V((2, D - 1, PN, LANES), BF16),
        *[V((DB, PN, B), BF16)] * H, V((A, SB, PN, B), BF16), V((3, SB, PN, B), BF16), V((3, D - 1, BPZ, PN, B), BF16),
        V((A, SB, PN, B), F32), V((D - 1, A, BPZ, PN, B), F32), V((7, PN, W), F32),
        dma,
        dma((H, S - 1)), dma((H, S - 1)), dma((3, D - 1)), dma((3, D - 1)),
        dma((D - 1,)), dma((D - 1,)), dma((D - 1,)), dma((D - 1,)),
        dma((2, D - 1)), dma((2, D - 1)),
        dma((H, S - 1)), dma((H, S - 1)), dma((H, D - 1)), dma((H, D - 1)),
    ]
    flops = 2 * H * 2 * A * K * PN * B * B
    return pl.pallas_call(
        functools.partial(kernel, S, D, N, B, BPZ, A, K),
        out_shape=(
            jax.ShapeDtypeStruct(logits.shape, F32),
            jax.ShapeDtypeStruct((PN, W), F32),
            jax.ShapeDtypeStruct((PN, W), F32),
        ),
        in_specs=[vmem, vmem, vmem, vmem, smem, pl.BlockSpec(memory_space=pl.ANY), smem, smem, smem],
        out_specs=(vmem, vmem, vmem),
        scratch_shapes=scratch,
        cost_estimate=pl.CostEstimate(flops=flops, bytes_accessed=tiles.size * 2, transcendentals=0),
        compiler_params=pltpu.CompilerParams(
            collective_id=0, has_side_effects=True, vmem_limit_bytes=48 * 1024 * 1024),
    )(density0, logits, value_final, base_reward, crowd, tiles.reshape(A * K * B, B), tile_src, tile_dst, tile_count)


def solution(mesh):
    in_specs = (
        P(None, ("src", "dst")),
        P(None, None, ("src", "dst")),
        P(None, ("src", "dst")),
        P(None, None, ("src", "dst")),
        P(),
        P("src", "dst", None, None, None, None),
        P("src", "dst", None, None),
        P("src", "dst", None, None),
        P("src", "dst", None),
    )
    out_specs = (P(None, None, ("src", "dst")), P(None, ("src", "dst")), P(None, ("src", "dst")))
    return jax.shard_map(body, mesh=mesh, in_specs=in_specs, out_specs=out_specs, check_vma=False)
```

time: 358 us -> 89.1 us (0.25)
  blocking collectives: 247 us -> 0 us
  Pallas kernels: 0 us -> 77.9 us
  waiting for transfers between devices: 62.4 us -> 0 us
  between operations: 14.4 us -> 0.66 us
  other arithmetic: 12.7 us -> 0 us
  matrix products: 9.69 us -> 0 us
    psum x4 -> x0, blocking collectives: 154 us -> none  [body(): population_mass = lax.psum(jnp.sum(arrived, axis=1), ('src', 'dst'))]
    all_gather x8 -> x0, blocking collectives: 92.8 us -> none  [the longest x4 58.8 us: body(): gathered = lax.all_gather(weighted, 'dst', axis=2, tiled=True)]
    pallas_call x0 -> x1, Pallas kernels: none -> 77.9 us  [body(): pl.pallas_call(functools.partial(kernel, S, D, N, B, BPZ, A, K), out_shap...]
    reduce_scatter x8 -> x0, waiting for transfers between devices: 62.3 us -> none  [the longest x4 62.2 us: body(): summed = lax.psum_scatter(returned, 'dst', scatter_dimension=2, tiled=True)]
    dot_general x16 -> x0, matrix products: 9.69 us -> none  [the longest x4 3.02 us: body(): jnp.einsum('aks,apki->apsi', to_src, product, precision=lax.Precision.HIG...]
    unnamed x20 -> x21, local copies, waits for them, and re-layouts: 2.83 us -> 9.3 us
    reduce_sum x7 -> x0, other arithmetic: 6.4 us -> none  [the longest x3 3.83 us: body(): value_next = jnp.sum(policy_now * evaluate_action_value, axis=0)]
    gather x9 -> x0, local copies, waits for them, and re-layouts: 4.64 us -> none  [the longest x5 2.41 us: take_rows(): return jnp.take(block_set, row_index, axis=1)]
  transfers between devices with their start and end apart: 8 -> 0, of which waited for: 4 -> 0; matrix products, arithmetic and copies ran while one was open for 3% -> 0% of each run, Pallas kernels for 0% -> 0%
where the time goes in v1:
time: 89.1 us; the launch traced here: 87.9 us
  Pallas kernels  77.9 us (87%)
  local copies, waits for them, and re-layouts  9.3 us (10%)
    pallas_call x1, Pallas kernels, body(): pl.pallas_call(functools.partial(kernel, S, D, N, B, BPZ, A, K), out_shap...  77.9 us
    unnamed x21, local copies, waits for them, and re-layouts  9.3 us

profile of v1, /device:TPU:0, one launch (start us, length us, event | category | flops | bytes accessed | tf_op | source)
XLA Modules:
  0.0 87.9 jit_solution(1784933331591830227)
XLA Ops:
  0.6 0.0 copy-start
  0.6 1.6 %copy-done = bf16[1,1,2,8,256,256]{5,4,3,2,1,0:T(8,128)(2,1)S(1)} copy-done((bf16[1,1,2,8,256,256]{5,4,3,2,1,0:T(8,128)(2,1)S(1)}, bf16[1,1,2,8,256,256]{5,4,3,2,1,0:T(8,128)(2,1)}, u32[]{:S(2)}) %copy-start) | copy-done | bytes 2097176
  2.2 0.0 copy-start.1
  2.2 0.8 copy-done.1
  3.1 0.0 copy-start.2
  3.1 0.8 copy-done.2
  3.9 0.0 copy-start.3
  3.9 0.8 copy-done.3
  4.7 0.0 copy-start.4
  4.7 0.8 copy-done.4
  5.4 0.0 copy-start.5
  5.4 0.7 copy-done.5
  6.1 0.0 copy-start.6
  6.1 0.7 copy-done.6
  6.8 0.0 copy-start.7
  6.8 0.7 copy-done.7
  7.4 0.0 copy-start.8
  7.4 0.7 copy-done.8
  8.1 77.9 %shard_map.112 = (f32[2,16,512]{2,1,0:T(8,128)S(1)}, f32[16,512]{1,0:T(8,128)S(1)}, f32[16,512]{1,0:T(8,128)S(1)}) custom-call(f32[16,512]{1,0:T(8,128)S(1)} %copy-done.3, f32[2,16,512]{2,1,0:T(8,128)S(1)} %copy-done.1, f32[16,512]{1,0:T(8,128)S(1)} %copy-done.4, f32[2,16,512]{2,1,0:T(8,128)S(1)} %copy-done.2, f32[16]{0:T(128)S(1)} %copy-done.7, ...), custom_call_target="tpu_custom_call" | custom-call | flops 268435456 | bytes 2097152 | tf_op jit(solution)/shard_map/pallas_call | solution.py:328
  86.0 0.6 copy.15
  86.6 0.6 copy.16
  87.3 0.6 copy.17
Async XLA Ops:
  0.6 1.6 %copy-start = (bf16[1,1,2,8,256,256]{5,4,3,2,1,0:T(8,128)(2,1)S(1)}, bf16[1,1,2,8,256,256]{5,4,3,2,1,0:T(8,128)(2,1)}, u32[]{:S(2)}) copy-start(bf16[1,1,2,8,256,256]{5,4,3,2,1,0:T(8,128)(2,1)} %param.14) | copy-start | bytes 6291460
  2.2 0.8 copy-start.1
  3.1 0.8 copy-start.2
  3.9 0.8 copy-start.3
  4.7 0.8 copy-start.4
  5.4 0.7 copy-start.5
  6.1 0.7 copy-start.6
  6.8 0.7 copy-start.7
  7.4 0.7 copy-start.8

commit v2 on v1

v2 whole, which is shorter than its diff:
```python
import functools

import jax
import jax.numpy as jnp
from jax import lax
from jax.experimental import pallas as pl
from jax.experimental.pallas import tpu as pltpu
from jax.sharding import PartitionSpec as P

H = 4
LANES = 128
DISCOUNT = 0.9
STEP_SIZE = 1.0
MESH = pl.DeviceIdType.MESH
F32 = jnp.float32
BF16 = jnp.bfloat16


def kernel(
    S, D, N, B, BPZ, A, K,
    density0_h, logits_h, value_final_h, base_reward_h, crowd_h, tiles_h, tile_src_h, tile_dst_h, tile_count_h,
    result,
    density0, logits, value_final, base_reward, crowd, tiles, tile_src, tile_dst, tile_count, in_sem,
    wbuf, w0buf, pol, margin, lhs, mask, prod, arr,
    rs_send, rs_recv, rz_send, rz_recv, ag_send, ag_recv, ag3_send, ag3_recv, ms_send, ms_recv,
    vb0, vb1, vb2, vb3, pr_send, pr_recv, zs_send, zs_recv, zl_send, zl_recv, keep, own,
    rs_ss, rs_rs, sh_ss, sh_rs, ms_ss, ms_rs, va_ss, va_rs, pr_ss, pr_rs, zs_ss, zs_rs,
):
    vbuf = (vb0, vb1, vb2, vb3)
    s = lax.axis_index("src")
    d = lax.axis_index("dst")
    Z = D // 2
    z = d // 2
    core = d - 2 * z
    PN, W = density0.shape
    src_peers = [lax.rem(s + r, S) for r in range(S)]
    dst_peers = [lax.rem(d + r, D) for r in range(D)]
    z_peers = [lax.rem(z + r, Z) for r in range(Z)]
    z_back = [lax.rem(z + Z - r, Z) for r in range(Z)]

    def remote(src, dst, ss, rs, device):
        return pltpu.make_async_remote_copy(
            src_ref=src, dst_ref=dst, send_sem=ss, recv_sem=rs, device_id=device, device_id_type=MESH)

    def to_src(src, dst, ss, rs, r):
        return remote(src, dst, ss, rs, (src_peers[r], d))

    def to_dst(src, dst, ss, rs, r):
        return remote(src, dst, ss, rs, (s, dst_peers[r]))

    def to_z(src, dst, ss, rs, r):
        return remote(src, dst, ss, rs, (s, 2 * z_peers[r] + core))

    def to_pair(src, dst, ss, rs):
        return remote(src, dst, ss, rs, (s, 2 * z + 1 - core))

    loads = [pltpu.make_async_copy(h, v, in_sem.at[i]) for i, (h, v) in enumerate((
        (logits_h, logits), (density0_h, density0), (value_final_h, value_final), (tile_src_h, tile_src),
        (tile_dst_h, tile_dst), (tile_count_h, tile_count), (crowd_h, crowd), (base_reward_h, base_reward),
        (tiles_h, tiles)))]
    for load in loads:
        load.start()
    barrier = pltpu.get_barrier_semaphore()
    for r in range(1, S):
        pl.semaphore_signal(barrier, inc=1, device_id=(src_peers[r], d), device_id_type=MESH)
    for r in range(1, D):
        pl.semaphore_signal(barrier, inc=1, device_id=(s, dst_peers[r]), device_id_type=MESH)

    for load in loads[:3]:
        load.wait()
    gap = logits[0] - logits[1]
    p0, p1 = jax.nn.sigmoid(gap), jax.nn.sigmoid(-gap)
    rho = density0[...]
    vf = value_final[...].astype(BF16)
    for b in range(BPZ):
        cols = slice(b * B, (b + 1) * B)
        w0buf[0, BPZ * d + b] = (p0 * rho)[:, cols].astype(BF16)
        w0buf[1, BPZ * d + b] = (p1 * rho)[:, cols].astype(BF16)
        margin[BPZ * d + b] = gap[:, cols]
        vbuf[3][BPZ * s + b] = vf[:, cols]
    pl.semaphore_wait(barrier, S + D - 2)

    pending = []

    def start(copy):
        copy.start()
        pending.append(copy)
        return copy

    def share(i, own_ref, there):
        ss, rs = sh_ss.at[i], sh_rs.at[i]
        hops = [start(to_z(own_ref, there(r), ss.at[r - 1], rs.at[r - 1], r)) for r in range(1, Z)]
        return hops, start(to_pair(own_ref, there(Z), ss.at[Z - 1], rs.at[Z - 1]))

    def relay(i, shared, here, there):
        ss, rs = sh_ss.at[i], sh_rs.at[i]
        hops, pair = shared
        onward = []
        for r in range(1, Z):
            hops[r - 1].wait_recv()
            onward.append(start(to_pair(here(r), there(r), ss.at[Z - 1 + r], rs.at[Z - 1 + r])))
        pair.wait_recv()
        for copy in onward:
            copy.wait_recv()

    def blocks_of(j):
        return pl.ds(BPZ * j, BPZ)

    def came_from(i):
        return 2 * z_back[i % Z] + (core if i < Z else 1 - core)

    def share_value(t):
        at = vbuf[t].at[pl.ds(BPZ * s, BPZ)]
        return [start(to_src(at, at, va_ss.at[t, r - 1], va_rs.at[t, r - 1], r)) for r in range(1, S)]

    w0_mine = w0buf.at[:, blocks_of(d)]
    w0_here = lambda r: w0buf.at[:, blocks_of(2 * z_back[r] + core)]
    w0 = share(0, w0_mine, lambda r: w0_mine)
    va = {3: share_value(3)}

    for load in loads[3:7]:
        load.wait()
    for a in range(A):
        for k in range(K):
            live = jnp.where(k < tile_count[0, 0, a], 1.0, 0.0).astype(F32)
            for c in range(BPZ * S):
                hit = jnp.where(tile_dst[0, 0, a, k] == c, live, 0.0)
                mask[(a * K + k) * BPZ * S + c] = jnp.full((PN, LANES), hit, F32).astype(BF16)
    row = lax.broadcasted_iota(jnp.int32, (PN, W), 0)
    crowd_col = jnp.zeros((PN, W), F32)
    for p in range(PN):
        crowd_col = jnp.where(row == p, crowd[p], crowd_col)
    own[4] = crowd_col
    own[5] = p0
    own[6] = p1
    lane = lax.broadcasted_iota(jnp.int32, (PN, LANES), 1)
    DB = BPZ * S

    def push(t):
        for a in range(A):
            for k in range(K):
                w = (w0buf if t == 0 else wbuf)[a, tile_src[0, 0, a, k]]
                q = a * K + k
                for c in range(DB):
                    m = mask[q * DB + c]
                    lhs[c * PN:(c + 1) * PN, q * B:(q + 1) * B] = w * jnp.concatenate([m] * (B // LANES), axis=1)
        arrived = jnp.dot(lhs[...], tiles[...], preferred_element_type=F32)
        total = arrived[0:PN]
        for c in range(1, DB):
            total = total + arrived[c * PN:(c + 1) * PN]
        mass = jnp.broadcast_to(jnp.sum(total, axis=1, keepdims=True), (PN, LANES))
        hi = mass.astype(BF16).astype(F32)
        mid = (mass - hi).astype(BF16).astype(F32)
        low = mass - hi - mid
        packed = jnp.where(lane == 3 * s, hi, jnp.where(lane == 3 * s + 1, mid, jnp.where(lane == 3 * s + 2, low, 0.0)))
        send, recv = (rs_send, rs_recv) if t == 0 else (rz_send.at[t - 1], rz_recv.at[t - 1])
        for c in range(DB):
            part = arrived[c * PN:(c + 1) * PN]
            at = slice((c % BPZ) * B, (c % BPZ + 1) * B)
            arr[c // BPZ, :, at] = part
            send[c // BPZ, :, at] = part.astype(send.dtype)
        for c in range(S):
            send[c, :, W:W + LANES] = packed.astype(send.dtype)
        copies = [start(to_src(send.at[src_peers[r]], recv.at[r - 1], rs_ss.at[t, r - 1], rs_rs.at[t, r - 1], r))
                  for r in range(1, S)]
        return copies, recv, packed.astype(BF16).astype(F32)

    def owned(pushed):
        copies, recv, packed = pushed
        raw = arr[s]
        for r in range(1, S):
            copies[r - 1].wait_recv()
            raw = raw + recv[r - 1, :, :W].astype(F32)
            packed = packed + recv[r - 1, :, W:W + LANES].astype(F32)
        return raw, packed

    def scale_of(packed):
        mass = jnp.sum(packed, axis=1, keepdims=True)
        return N / mass

    def weigh(block, raw, scale):
        now = raw * scale
        wbuf[0, block] = (pol[0, block] * now).astype(BF16)
        wbuf[1, block] = (pol[1, block] * now).astype(BF16)

    def share_density(t, raw, packed):
        ag_send[t, :, :W] = raw.astype(BF16)
        ag_send[t, :, W:W + LANES] = packed.astype(BF16)
        return share(2 + t, ag_send.at[t], lambda r: ag_recv.at[t, r])

    def take_density(t, raw, packed, shared):
        slot = lambda r: ag_recv.at[t, r]
        relay(2 + t, shared, slot, lambda r: ag_recv.at[t, Z + r])
        for i in range(1, 2 * Z):
            packed = packed + ag_recv[t, i, :, W:W + LANES].astype(F32)
        scale = scale_of(packed)
        for b in range(BPZ):
            weigh(BPZ * d + b, raw[:, b * B:(b + 1) * B], scale)
        for i in range(1, 2 * Z):
            for b in range(BPZ):
                weigh(BPZ * came_from(i) + b, ag_recv[t, i, :, b * B:(b + 1) * B].astype(F32), scale)
        return raw * scale

    def send_mass(i, packed):
        ms_send[i] = packed.astype(BF16)
        return [start(to_dst(ms_send.at[i], ms_recv.at[i, r - 1], ms_ss.at[i, r - 1], ms_rs.at[i, r - 1], r))
                for r in range(1, D)]

    def take_mass(i, packed, copies):
        for r in range(1, D):
            copies[r - 1].wait_recv()
            packed = packed + ms_recv[i, r - 1].astype(F32)
        return scale_of(packed)

    def collect(a, block):
        out = None
        for k in range(K):
            term = jnp.where(tile_src[0, 0, a, k] == block, 1.0, 0.0).astype(F32) * prod[a * K + k]
            out = term if out is None else out + term
        return out

    def parts(t, block):
        out = [collect(a, block) for a in range(A)]
        return out if t == 0 else [pol[0, block] * out[0] + pol[1, block] * out[1]]

    order = list(range(1, Z)) + [0]

    def pull(t):
        for copy in va[t]:
            copy.wait_recv()
        for a in range(A):
            for k in range(K):
                q = a * K + k
                v = vbuf[t][tile_dst[0, 0, a, k]]
                live = jnp.where(k < tile_count[0, 0, a], 1.0, 0.0).astype(F32)
                prod[q] = live * lax.dot_general(
                    v, tiles[q * B:(q + 1) * B, :], (((1,), (1,)), ((), ())), preferred_element_type=F32)
        n = A * BPZ if t == 0 else BPZ
        copies = {}
        for r in order:
            for b in range(BPZ):
                for i, part in enumerate(parts(t, BPZ * (2 * z_peers[r] + 1 - core) + b)):
                    pr_send[t, r, i * BPZ + b] = part
            copies[r] = start(to_pair(pr_send.at[t, r, pl.ds(0, n)], pr_recv.at[t, r, pl.ds(0, n)],
                                      pr_ss.at[t, r], pr_rs.at[t, r]))
        for r in order:
            for b in range(BPZ):
                for i, part in enumerate(parts(t, BPZ * (2 * z_peers[r] + core) + b)):
                    keep[t, r, i * BPZ + b] = part
        return copies

    def spread(t, copies):
        n = A * BPZ if t == 0 else BPZ
        send, recv = (zl_send, zl_recv) if t == 0 else (zs_send.at[t - 1], zs_recv.at[t - 1])
        out = []
        for r in order:
            copies[r].wait_recv()
            for m in range(n):
                both = keep[t, r, m] + pr_recv[t, r, m]
                if r == 0:
                    keep[t, r, m] = both
                else:
                    send[r - 1, m] = both.astype(send.dtype)
            if r:
                out.append(start(to_z(send.at[r - 1], recv.at[r - 1], zs_ss.at[t, r - 1], zs_rs.at[t, r - 1], r)))
        return out

    def summed(t, m):
        recv = zl_recv if t == 0 else zs_recv.at[t - 1]
        total = keep[t, 0, m]
        for r in range(1, Z):
            total = total + recv[r - 1, m].astype(F32)
        return total

    def crowding(t, now):
        own[t] = own[4] * jnp.log(1.0 + jnp.mean(now, axis=0, keepdims=True))

    def next_value(t, copies):
        reward = []
        for b in range(BPZ):
            cols = slice(b * B, (b + 1) * B)
            q0, q1 = own[5, :, cols], own[6, :, cols]
            reward.append(q0 * base_reward[0, :, cols] + q1 * base_reward[1, :, cols] - (q0 + q1) * own[t, :, cols])
        for copy in copies:
            copy.wait_recv()
        for b in range(BPZ):
            vbuf[t - 1][BPZ * s + b] = (reward[b] + DISCOUNT * summed(t, b)).astype(BF16)
        va[t - 1] = share_value(t - 1)

    relay(0, w0, w0_here, w0_here)
    mg_mine = margin.at[blocks_of(d)]
    mg_here = lambda r: margin.at[blocks_of(2 * z_back[r] + core)]
    mg = share(1, mg_mine, lambda r: mg_mine)
    for load in loads[7:]:
        load.wait()
    pushed = push(0)
    crowding(0, rho)
    relay(1, mg, mg_here, mg_here)

    def policy(g, _):
        for b in range(BPZ):
            c = g * BPZ + b
            pol[0, c] = jax.nn.sigmoid(margin[c])
            pol[1, c] = jax.nn.sigmoid(-margin[c])
        return _

    lax.fori_loop(0, D, policy, 0)
    raw, packed = owned(pushed)
    shared = share_density(0, raw, packed)
    now = take_density(0, raw, packed, shared)
    pushed = push(1)
    crowding(1, now)
    pr = pull(3)
    raw, packed = owned(pushed)
    shared = share_density(1, raw, packed)
    now = take_density(1, raw, packed, shared)
    pushed = push(2)
    crowding(2, now)
    zs = spread(3, pr)
    raw, packed = owned(pushed)
    ms = send_mass(0, packed)
    ag3_send[...] = raw
    scale3 = take_mass(0, packed, ms)
    now = raw * scale3
    crowding(3, now)
    next_value(3, zs)
    shared = share(4, ag3_send, lambda r: ag3_recv.at[r])
    pr = pull(2)
    zs = spread(2, pr)
    relay(4, shared, lambda r: ag3_recv.at[r], lambda r: ag3_recv.at[Z + r])
    for b in range(BPZ):
        weigh(BPZ * d + b, raw[:, b * B:(b + 1) * B], scale3)
        for i in range(1, 2 * Z):
            weigh(BPZ * came_from(i) + b, ag3_recv[i, :, b * B:(b + 1) * B], scale3)
    next_value(2, zs)
    pushed = push(3)
    pr = pull(1)
    zs = spread(1, pr)
    raw, packed = owned(pushed)
    ms = send_mass(1, packed)
    next_value(1, zs)
    result[A + 1] = raw * take_mass(1, packed, ms)
    pr = pull(0)
    zs = spread(0, pr)
    for copy in zs:
        copy.wait_recv()
    for b in range(BPZ):
        cols = slice(b * B, (b + 1) * B)
        value = None
        for a in range(A):
            action_value = base_reward[a, :, cols] - own[0, :, cols] + DISCOUNT * summed(0, a * BPZ + b)
            result[a, :, cols] = logits[a, :, cols] + STEP_SIZE * action_value
            term = own[5 + a, :, cols] * action_value
            value = term if value is None else value + term
        result[A, :, cols] = value
    for copy in pending:
        copy.wait_send()


def body(density0, logits, value_final, base_reward, crowd, tiles, tile_src, tile_dst, tile_count):
    S, D = lax.axis_size("src"), lax.axis_size("dst")
    PN, W = density0.shape
    A, K, B = tiles.shape[2], tiles.shape[3], tiles.shape[-1]
    BPZ = W // B
    SB, DB, Z = BPZ * D, BPZ * S, D // 2
    N = float(W * S * D)
    dma = pltpu.SemaphoreType.DMA
    V = pltpu.VMEM
    args = (density0, logits, value_final, base_reward, crowd, tiles.reshape(A * K * B, B), tile_src, tile_dst, tile_count)
    places = (V, V, V, V, pltpu.SMEM, V, pltpu.SMEM, pltpu.SMEM, pltpu.SMEM)
    shared = dma((5, 2 * Z - 1))
    scratch = [place(x.shape, x.dtype) for place, x in zip(places, args)] + [
        dma((len(args),)),
        V((A, SB, PN, B), BF16), V((A, SB, PN, B), BF16), V((A, SB, PN, B), F32), V((SB, PN, B), F32),
        V((DB * PN, A * K * B), BF16), V((A * K * DB, PN, LANES), BF16), V((A * K, PN, B), F32), V((S, PN, W), F32),
        V((S, PN, W + LANES), BF16), V((S - 1, PN, W + LANES), BF16),
        V((H - 1, S, PN, W + LANES), F32), V((H - 1, S - 1, PN, W + LANES), F32),
        V((2, PN, W + LANES), BF16), V((2, 2 * Z, PN, W + LANES), BF16),
        V((PN, W), F32), V((2 * Z, PN, W), F32), V((2, PN, LANES), BF16), V((2, D - 1, PN, LANES), BF16),
        *[V((DB, PN, B), BF16)] * H,
        V((H, Z, A * BPZ, PN, B), F32), V((H, Z, A * BPZ, PN, B), F32),
        V((H - 1, Z - 1, BPZ, PN, B), BF16), V((H - 1, Z - 1, BPZ, PN, B), BF16),
        V((Z - 1, A * BPZ, PN, B), F32), V((Z - 1, A * BPZ, PN, B), F32),
        V((H, Z, A * BPZ, PN, B), F32), V((7, PN, W), F32),
        dma((H, S - 1)), dma((H, S - 1)), shared, shared, dma((2, D - 1)), dma((2, D - 1)),
        dma((H, S - 1)), dma((H, S - 1)), dma((H, Z)), dma((H, Z)), dma((H, Z - 1)), dma((H, Z - 1)),
    ]
    flops = 2 * H * 2 * A * K * PN * B * B
    out = pl.pallas_call(
        functools.partial(kernel, S, D, N, B, BPZ, A, K),
        out_shape=jax.ShapeDtypeStruct((A + 2, PN, W), F32),
        in_specs=[pl.BlockSpec(memory_space=pltpu.HBM)] * len(args),
        out_specs=pl.BlockSpec(memory_space=pltpu.VMEM),
        scratch_shapes=scratch,
        cost_estimate=pl.CostEstimate(flops=flops, bytes_accessed=tiles.size * 2, transcendentals=0),
        compiler_params=pltpu.CompilerParams(
            collective_id=0, has_side_effects=True, vmem_limit_bytes=62 * 1024 * 1024),
    )(*args)
    return out[:A], out[A], out[A + 1]


def solution(mesh):
    in_specs = (
        P(None, ("src", "dst")),
        P(None, None, ("src", "dst")),
        P(None, ("src", "dst")),
        P(None, None, ("src", "dst")),
        P(),
        P("src", "dst", None, None, None, None),
        P("src", "dst", None, None),
        P("src", "dst", None, None),
        P("src", "dst", None),
    )
    out_specs = (P(None, None, ("src", "dst")), P(None, ("src", "dst")), P(None, ("src", "dst")))
    return jax.shard_map(body, mesh=mesh, in_specs=in_specs, out_specs=out_specs, check_vma=False)
```

time: 89.1 us -> 74.9 us (0.84); the launches traced: 87.9 us -> 74.7 us
  Pallas kernels: 77.9 us -> 71.1 us
  local copies, waits for them, and re-layouts: 9.3 us -> 2.88 us
    unnamed x21 -> x0, local copies, waits for them, and re-layouts: 9.3 us -> none
    pallas_call x1, Pallas kernels: 77.9 us -> 71.1 us  [body(): pl.pallas_call(functools.partial(kernel, S, D, N, B, BPZ, A, K), out_shap...]
    slice x0 -> x1, local copies, waits for them, and re-layouts: none -> 1.47 us  [body(): return (out[:A], out[A], out[A + 1])]
    squeeze x0 -> x1, local copies, waits for them, and re-layouts: none -> 1.41 us  [body(): return (out[:A], out[A], out[A + 1])]
where the time goes in v2:
time: 74.9 us; the launch traced here: 74.7 us
  Pallas kernels  71.1 us (95%)
  local copies, waits for them, and re-layouts  2.88 us (4%)
    pallas_call x1, Pallas kernels, body(): pl.pallas_call(functools.partial(kernel, S, D, N, B, BPZ, A, K), out_shap...  71.1 us

profile of v2, /device:TPU:0, one launch (start us, length us, event | category | flops | bytes accessed | tf_op | source)
XLA Modules:
  0.0 74.7 jit_solution(17876515133151924276)
XLA Ops:
  0.6 71.1 %shard_map.112 = f32[4,16,512]{2,1,0:T(8,128)} custom-call(f32[16,512]{1,0:T(8,128)} %density0_h.1, f32[2,16,512]{2,1,0:T(8,128)} %logits_h.1, f32[16,512]{1,0:T(8,128)} %value_final_h.1, f32[2,16,512]{2,1,0:T(8,128)} %base_reward_h.1, f32[16]{0:T(128)} %crowd_h.1, bf16[4096,256]{1,0:T(8,128)(2,1)} %bitcast.5, s32[1,1,2,8]{3,2,1,0:T(2,128)} %tile_src_h.1, ...), custom_call_target="tpu_custom_call" | custom-call | flops 268435456 | bytes 2097152 | tf_op jit(solution)/shard_map/pallas_call | solution.py:389
  71.8 1.4 %slice_bitcast_fusion = (f32[16,512]{1,0:T(8,128)}, f32[16,512]{1,0:T(8,128)}) fusion(f32[4,16,512]{2,1,0:T(8,128)} %shard_map.112), kind=kLoop, calls=%fused_computation | loop fusion | bytes 131072 | tf_op jit(solution)/shard_map/squeeze | solution.py:399
  73.2 1.5 %slice.9 = f32[2,16,512]{2,1,0:T(8,128)} slice(f32[4,16,512]{2,1,0:T(8,128)} %shard_map.112), slice={[0:2], [0:16], [0:512]} | slice | bytes 131072 | tf_op jit(solution)/shard_map/slice | solution.py:399

commit v3 on v2

--- a/solution.py
+++ b/solution.py
@@ -21,9 +21,9 @@
     density0_h, logits_h, value_final_h, base_reward_h, crowd_h, tiles_h, tile_src_h, tile_dst_h, tile_count_h,
     result,
     density0, logits, value_final, base_reward, crowd, tiles, tile_src, tile_dst, tile_count, in_sem,
-    wbuf, w0buf, pol, margin, lhs, mask, prod, arr,
+    turned, wbuf, w0buf, pol, margin, lhs, mask, prod, arr,
     rs_send, rs_recv, rz_send, rz_recv, ag_send, ag_recv, ag3_send, ag3_recv, ms_send, ms_recv,
-    vb0, vb1, vb2, vb3, pr_send, pr_recv, zs_send, zs_recv, zl_send, zl_recv, keep, own,
+    vb0, vb1, vb2, vb3, pr_send, pr_recv, zs_send, zs_recv, zl_send, zl_recv, zh_send, zh_recv, keep, own,
     rs_ss, rs_rs, sh_ss, sh_rs, ms_ss, ms_rs, va_ss, va_rs, pr_ss, pr_rs, zs_ss, zs_rs,
 ):
     vbuf = (vb0, vb1, vb2, vb3)
@@ -153,7 +153,7 @@
         mid = (mass - hi).astype(BF16).astype(F32)
         low = mass - hi - mid
         packed = jnp.where(lane == 3 * s, hi, jnp.where(lane == 3 * s + 1, mid, jnp.where(lane == 3 * s + 2, low, 0.0)))
-        send, recv = (rs_send, rs_recv) if t == 0 else (rz_send.at[t - 1], rz_recv.at[t - 1])
+        send, recv = (rs_send.at[t], rs_recv.at[t]) if t < 2 else (rz_send.at[t - 2], rz_recv.at[t - 2])
         for c in range(DB):
             part = arrived[c * PN:(c + 1) * PN]
             at = slice((c % BPZ) * B, (c % BPZ + 1) * B)
@@ -233,8 +233,7 @@
                 q = a * K + k
                 v = vbuf[t][tile_dst[0, 0, a, k]]
                 live = jnp.where(k < tile_count[0, 0, a], 1.0, 0.0).astype(F32)
-                prod[q] = live * lax.dot_general(
-                    v, tiles[q * B:(q + 1) * B, :], (((1,), (1,)), ((), ())), preferred_element_type=F32)
+                prod[q] = live * jnp.dot(v, turned[q * B:(q + 1) * B, :], preferred_element_type=F32)
         n = A * BPZ if t == 0 else BPZ
         copies = {}
         for r in order:
@@ -251,7 +250,7 @@
 
     def spread(t, copies):
         n = A * BPZ if t == 0 else BPZ
-        send, recv = (zl_send, zl_recv) if t == 0 else (zs_send.at[t - 1], zs_recv.at[t - 1])
+        sends = last_sends if t == 0 else [(zs_send.at[t - 1], zs_recv.at[t - 1], t)]
         out = []
         for r in order:
             copies[r].wait_recv()
@@ -260,16 +259,25 @@
                 if r == 0:
                     keep[t, r, m] = both
                 else:
-                    send[r - 1, m] = both.astype(send.dtype)
+                    i, at = last_place(m) if t == 0 else (0, m)
+                    sends[i][0][r - 1, at] = both.astype(sends[i][0].dtype)
             if r:
-                out.append(start(to_z(send.at[r - 1], recv.at[r - 1], zs_ss.at[t, r - 1], zs_rs.at[t, r - 1], r)))
+                for send, recv, row in sends:
+                    out.append(start(to_z(send.at[r - 1], recv.at[r - 1], zs_ss.at[row, r - 1], zs_rs.at[row, r - 1], r)))
         return out
 
+    last_sends = [(zl_send, zl_recv, 0), (zh_send, zh_recv, H)]
+
+    def last_place(m):
+        a, b = m // BPZ, m % BPZ
+        return b % 2, a * (BPZ // 2 if b % 2 else BPZ - BPZ // 2) + b // 2
+
     def summed(t, m):
-        recv = zl_recv if t == 0 else zs_recv.at[t - 1]
+        i, at = last_place(m) if t == 0 else (0, m)
+        recv = last_sends[i][1] if t == 0 else zs_recv.at[t - 1]
         total = keep[t, 0, m]
         for r in range(1, Z):
-            total = total + recv[r - 1, m].astype(F32)
+            total = total + recv[r - 1, at].astype(F32)
         return total
 
     def crowding(t, now):
@@ -287,12 +295,19 @@
             vbuf[t - 1][BPZ * s + b] = (reward[b] + DISCOUNT * summed(t, b)).astype(BF16)
         va[t - 1] = share_value(t - 1)
 
+    for load in loads[7:]:
+        load.wait()
+
+    def turn(q, _):
+        at = pl.ds(pl.multiple_of(q * B, B), B)
+        turned[at, :] = tiles[at, :].T
+        return _
+
+    lax.fori_loop(0, A * K, turn, 0)
     relay(0, w0, w0_here, w0_here)
     mg_mine = margin.at[blocks_of(d)]
     mg_here = lambda r: margin.at[blocks_of(2 * z_back[r] + core)]
     mg = share(1, mg_mine, lambda r: mg_mine)
-    for load in loads[7:]:
-        load.wait()
     pushed = push(0)
     crowding(0, rho)
     relay(1, mg, mg_here, mg_here)
@@ -357,6 +372,15 @@
         copy.wait_send()
 
 
+def deliver(A, result, new_logits, value_start, density_final, sem):
+    parts = ((result.at[pl.ds(0, A)], new_logits), (result.at[A], value_start), (result.at[A + 1], density_final))
+    copies = [pltpu.make_async_copy(part, out, sem.at[i]) for i, (part, out) in enumerate(parts)]
+    for copy in copies:
+        copy.start()
+    for copy in copies:
+        copy.wait()
+
+
 def body(density0, logits, value_final, base_reward, crowd, tiles, tile_src, tile_dst, tile_count):
     S, D = lax.axis_size("src"), lax.axis_size("dst")
     PN, W = density0.shape
@@ -370,20 +394,21 @@
     places = (V, V, V, V, pltpu.SMEM, V, pltpu.SMEM, pltpu.SMEM, pltpu.SMEM)
     shared = dma((5, 2 * Z - 1))
     scratch = [place(x.shape, x.dtype) for place, x in zip(places, args)] + [
-        dma((len(args),)),
+        dma((len(args),)), V((A * K * B, B), BF16),
         V((A, SB, PN, B), BF16), V((A, SB, PN, B), BF16), V((A, SB, PN, B), F32), V((SB, PN, B), F32),
         V((DB * PN, A * K * B), BF16), V((A * K * DB, PN, LANES), BF16), V((A * K, PN, B), F32), V((S, PN, W), F32),
-        V((S, PN, W + LANES), BF16), V((S - 1, PN, W + LANES), BF16),
-        V((H - 1, S, PN, W + LANES), F32), V((H - 1, S - 1, PN, W + LANES), F32),
+        V((2, S, PN, W + LANES), BF16), V((2, S - 1, PN, W + LANES), BF16),
+        V((H - 2, S, PN, W + LANES), F32), V((H - 2, S - 1, PN, W + LANES), F32),
         V((2, PN, W + LANES), BF16), V((2, 2 * Z, PN, W + LANES), BF16),
         V((PN, W), F32), V((2 * Z, PN, W), F32), V((2, PN, LANES), BF16), V((2, D - 1, PN, LANES), BF16),
         *[V((DB, PN, B), BF16)] * H,
         V((H, Z, A * BPZ, PN, B), F32), V((H, Z, A * BPZ, PN, B), F32),
         V((H - 1, Z - 1, BPZ, PN, B), BF16), V((H - 1, Z - 1, BPZ, PN, B), BF16),
-        V((Z - 1, A * BPZ, PN, B), F32), V((Z - 1, A * BPZ, PN, B), F32),
+        V((Z - 1, A * (BPZ - BPZ // 2), PN, B), F32), V((Z - 1, A * (BPZ - BPZ // 2), PN, B), F32),
+        V((Z - 1, A * (BPZ // 2), PN, B), BF16), V((Z - 1, A * (BPZ // 2), PN, B), BF16),
         V((H, Z, A * BPZ, PN, B), F32), V((7, PN, W), F32),
         dma((H, S - 1)), dma((H, S - 1)), shared, shared, dma((2, D - 1)), dma((2, D - 1)),
-        dma((H, S - 1)), dma((H, S - 1)), dma((H, Z)), dma((H, Z)), dma((H, Z - 1)), dma((H, Z - 1)),
+        dma((H, S - 1)), dma((H, S - 1)), dma((H, Z)), dma((H, Z)), dma((H + 1, Z - 1)), dma((H + 1, Z - 1)),
     ]
     flops = 2 * H * 2 * A * K * PN * B * B
     out = pl.pallas_call(
@@ -396,7 +421,15 @@
         compiler_params=pltpu.CompilerParams(
             collective_id=0, has_side_effects=True, vmem_limit_bytes=62 * 1024 * 1024),
     )(*args)
-    return out[:A], out[A], out[A + 1]
+    hbm = pl.BlockSpec(memory_space=pltpu.HBM)
+    return pl.pallas_call(
+        functools.partial(deliver, A),
+        out_shape=(jax.ShapeDtypeStruct((A, PN, W), F32),) + (jax.ShapeDtypeStruct((PN, W), F32),) * 2,
+        in_specs=[hbm],
+        out_specs=(hbm,) * 3,
+        scratch_shapes=[dma((3,))],
+        compiler_params=pltpu.CompilerParams(vmem_limit_bytes=62 * 1024 * 1024),
+    )(out)
 
 
 def solution(mesh):

time: 74.9 us -> 74.5 us (level)
  local copies, waits for them, and re-layouts: 2.88 us -> 0 us
  Pallas kernels: 71.1 us -> 73.8 us
    pallas_call x0 -> x1, Pallas kernels: none -> 5.1 us  [body(): pl.pallas_call(functools.partial(deliver, A), out_shape=(jax.ShapeDtypeSt...]
    pallas_call x1, Pallas kernels: 71.1 us -> 68.7 us  [body(): pl.pallas_call(functools.partial(kernel, S, D, N, B, BPZ, A, K), out_shap...]
    slice x1 -> x0, local copies, waits for them, and re-layouts: 1.47 us -> none  [body(): return (out[:A], out[A], out[A + 1])]
    squeeze x1 -> x0, local copies, waits for them, and re-layouts: 1.41 us -> none  [body(): return (out[:A], out[A], out[A + 1])]
where the time goes in v3:
time: 74.5 us; the launch traced here: 74.4 us
  Pallas kernels  73.8 us (99%)
    pallas_call x1, Pallas kernels, body(): pl.pallas_call(functools.partial(kernel, S, D, N, B, BPZ, A, K), out_shap...  68.7 us
    pallas_call x1, Pallas kernels, body(): pl.pallas_call(functools.partial(deliver, A), out_shape=(jax.ShapeDtypeSt...  5.1 us

profile of v3, /device:TPU:0, one launch (start us, length us, event | category | flops | bytes accessed | tf_op | source)
XLA Modules:
  0.0 74.4 jit_solution(9263962986883553660)
XLA Ops:
  0.6 68.7 %shard_map.112.result = f32[4,16,512]{2,1,0:T(8,128)} custom-call(f32[16,512]{1,0:T(8,128)} %density0_h.1, f32[2,16,512]{2,1,0:T(8,128)} %logits_h.1, f32[16,512]{1,0:T(8,128)} %value_final_h.1, f32[2,16,512]{2,1,0:T(8,128)} %base_reward_h.1, f32[16]{0:T(128)} %crowd_h.1, bf16[4096,256]{1,0:T(8,128)(2,1)} %bitcast.1, s32[1,1,2,8]{3,2,1,0:T(2,128)} %tile_src_h.1, ...), custom_call_target="tpu_custom_call" | custom-call | flops 268435456 | bytes 2097152 | tf_op jit(solution)/shard_map/pallas_call | solution.py:414
  69.3 5.1 %shard_map.113 = (f32[2,16,512]{2,1,0:T(8,128)}, f32[16,512]{1,0:T(8,128)}, f32[16,512]{1,0:T(8,128)}) custom-call(f32[4,16,512]{2,1,0:T(8,128)} %shard_map.112.result), custom_call_target="tpu_custom_call" | custom-call | tf_op jit(solution)/shard_map/pallas_call | solution.py:425

commit v4 on v3

--- a/solution.py
+++ b/solution.py
@@ -23,8 +23,8 @@
     density0, logits, value_final, base_reward, crowd, tiles, tile_src, tile_dst, tile_count, in_sem,
     turned, wbuf, w0buf, pol, margin, lhs, mask, prod, arr,
     rs_send, rs_recv, rz_send, rz_recv, ag_send, ag_recv, ag3_send, ag3_recv, ms_send, ms_recv,
-    vb0, vb1, vb2, vb3, pr_send, pr_recv, zs_send, zs_recv, zl_send, zl_recv, zh_send, zh_recv, keep, own,
-    rs_ss, rs_rs, sh_ss, sh_rs, ms_ss, ms_rs, va_ss, va_rs, pr_ss, pr_rs, zs_ss, zs_rs,
+    vb0, vb1, vb2, vb3, pr_send, pr_recv, zs_send, zs_recv, zl_send, zl_recv, zh_send, zh_recv, row_send, row_recv, col_send, col_recv, keep, own,
+    rs_ss, rs_rs, sh_ss, sh_rs, ms_ss, ms_rs, va_ss, va_rs, pr_ss, pr_rs, zs_ss, zs_rs, row_ss, row_rs, col_ss, col_rs,
 ):
     vbuf = (vb0, vb1, vb2, vb3)
     s = lax.axis_index("src")
@@ -136,6 +136,13 @@
     lane = lax.broadcasted_iota(jnp.int32, (PN, LANES), 1)
     DB = BPZ * S
 
+    def pack(terms):
+        mass = jnp.broadcast_to(jnp.sum(terms, axis=1, keepdims=True), (PN, LANES))
+        hi = mass.astype(BF16).astype(F32)
+        mid = (mass - hi).astype(BF16).astype(F32)
+        low = (mass - hi - mid).astype(BF16).astype(F32)
+        return jnp.where(lane == 3 * s, hi, jnp.where(lane == 3 * s + 1, mid, jnp.where(lane == 3 * s + 2, low, 0.0)))
+
     def push(t):
         for a in range(A):
             for k in range(K):
@@ -148,11 +155,7 @@
         total = arrived[0:PN]
         for c in range(1, DB):
             total = total + arrived[c * PN:(c + 1) * PN]
-        mass = jnp.broadcast_to(jnp.sum(total, axis=1, keepdims=True), (PN, LANES))
-        hi = mass.astype(BF16).astype(F32)
-        mid = (mass - hi).astype(BF16).astype(F32)
-        low = mass - hi - mid
-        packed = jnp.where(lane == 3 * s, hi, jnp.where(lane == 3 * s + 1, mid, jnp.where(lane == 3 * s + 2, low, 0.0)))
+        packed = pack(total)
         send, recv = (rs_send.at[t], rs_recv.at[t]) if t < 2 else (rz_send.at[t - 2], rz_recv.at[t - 2])
         for c in range(DB):
             part = arrived[c * PN:(c + 1) * PN]
@@ -163,7 +166,7 @@
             send[c, :, W:W + LANES] = packed.astype(send.dtype)
         copies = [start(to_src(send.at[src_peers[r]], recv.at[r - 1], rs_ss.at[t, r - 1], rs_rs.at[t, r - 1], r))
                   for r in range(1, S)]
-        return copies, recv, packed.astype(BF16).astype(F32)
+        return copies, recv, packed
 
     def owned(pushed):
         copies, recv, packed = pushed
@@ -224,6 +227,38 @@
         return out if t == 0 else [pol[0, block] * out[0] + pol[1, block] * out[1]]
 
     order = list(range(1, Z)) + [0]
+
+    def row_sums():
+        ones = jnp.ones((PN, B), BF16)
+        for a in range(A):
+            for k in range(K):
+                q = a * K + k
+                live = jnp.where(k < tile_count[0, 0, a], 1.0, 0.0).astype(F32)
+                prod[q] = live * jnp.dot(ones, turned[q * B:(q + 1) * B, :], preferred_element_type=F32)
+        rows = row_send.shape[1]
+        which = lax.broadcasted_iota(jnp.int32, (rows, B), 0)
+
+        def one(j, _):
+            out = jnp.zeros((rows, B), F32)
+            for m in range(A * BPZ):
+                part = collect(m // BPZ, BPZ * j + m % BPZ)[0:1]
+                out = jnp.where(which == m, jnp.broadcast_to(part, (rows, B)), out)
+            row_send[j] = out
+            return _
+
+        lax.fori_loop(0, D, one, 0)
+
+    def own_mass(now, copies):
+        total = row_send[d]
+        for r in range(1, D):
+            copies[r - 1].wait_recv()
+            total = total + row_recv[r - 1]
+        terms = jnp.zeros((PN, B), F32)
+        for m in range(A * BPZ):
+            cols = slice((m % BPZ) * B, (m % BPZ + 1) * B)
+            w = (own[5 + m // BPZ, :, cols] * now[:, cols]).astype(BF16).astype(F32)
+            terms = terms + w * total[m:m + 1]
+        return pack(terms)
 
     def pull(t):
         for copy in va[t]:
@@ -310,6 +345,9 @@
     mg = share(1, mg_mine, lambda r: mg_mine)
     pushed = push(0)
     crowding(0, rho)
+    row_sums()
+    raw, packed = owned(pushed)
+    shared = share_density(0, raw, packed)
     relay(1, mg, mg_here, mg_here)
 
     def policy(g, _):
@@ -320,20 +358,26 @@
         return _
 
     lax.fori_loop(0, D, policy, 0)
-    raw, packed = owned(pushed)
-    shared = share_density(0, raw, packed)
     now = take_density(0, raw, packed, shared)
     pushed = push(1)
+    row_copies = [start(to_dst(row_send.at[dst_peers[r]], row_recv.at[r - 1], row_ss.at[r - 1], row_rs.at[r - 1], r))
+                  for r in range(1, D)]
     crowding(1, now)
     pr = pull(3)
     raw, packed = owned(pushed)
     shared = share_density(1, raw, packed)
     now = take_density(1, raw, packed, shared)
+    packed = own_mass(now, row_copies)
+    col_send[...] = packed.astype(BF16)
+    col_copies = [start(to_src(col_send, col_recv.at[r - 1], col_ss.at[r - 1], col_rs.at[r - 1], r)) for r in range(1, S)]
     pushed = push(2)
+    for r in range(1, S):
+        col_copies[r - 1].wait_recv()
+        packed = packed + col_recv[r - 1].astype(F32)
+    ms = send_mass(0, packed)
     crowding(2, now)
     zs = spread(3, pr)
-    raw, packed = owned(pushed)
-    ms = send_mass(0, packed)
+    raw, _ = owned(pushed)
     ag3_send[...] = raw
     scale3 = take_mass(0, packed, ms)
     now = raw * scale3
@@ -372,13 +416,10 @@
         copy.wait_send()
 
 
-def deliver(A, result, new_logits, value_start, density_final, sem):
-    parts = ((result.at[pl.ds(0, A)], new_logits), (result.at[A], value_start), (result.at[A + 1], density_final))
-    copies = [pltpu.make_async_copy(part, out, sem.at[i]) for i, (part, out) in enumerate(parts)]
-    for copy in copies:
-        copy.start()
-    for copy in copies:
-        copy.wait()
+def deliver(A, result, new_logits, value_start, density_final):
+    new_logits[...] = result[:A]
+    value_start[...] = result[A]
+    density_final[...] = result[A + 1]
 
 
 def body(density0, logits, value_final, base_reward, crowd, tiles, tile_src, tile_dst, tile_count):
@@ -388,6 +429,7 @@
     BPZ = W // B
     SB, DB, Z = BPZ * D, BPZ * S, D // 2
     N = float(W * S * D)
+    rows = -(-A * BPZ // 8) * 8
     dma = pltpu.SemaphoreType.DMA
     V = pltpu.VMEM
     args = (density0, logits, value_final, base_reward, crowd, tiles.reshape(A * K * B, B), tile_src, tile_dst, tile_count)
@@ -406,9 +448,11 @@
         V((H - 1, Z - 1, BPZ, PN, B), BF16), V((H - 1, Z - 1, BPZ, PN, B), BF16),
         V((Z - 1, A * (BPZ - BPZ // 2), PN, B), F32), V((Z - 1, A * (BPZ - BPZ // 2), PN, B), F32),
         V((Z - 1, A * (BPZ // 2), PN, B), BF16), V((Z - 1, A * (BPZ // 2), PN, B), BF16),
+        V((D, rows, B), F32), V((D - 1, rows, B), F32), V((PN, LANES), BF16), V((S - 1, PN, LANES), BF16),
         V((H, Z, A * BPZ, PN, B), F32), V((7, PN, W), F32),
         dma((H, S - 1)), dma((H, S - 1)), shared, shared, dma((2, D - 1)), dma((2, D - 1)),
         dma((H, S - 1)), dma((H, S - 1)), dma((H, Z)), dma((H, Z)), dma((H + 1, Z - 1)), dma((H + 1, Z - 1)),
+        dma((D - 1,)), dma((D - 1,)), dma((S - 1,)), dma((S - 1,)),
     ]
     flops = 2 * H * 2 * A * K * PN * B * B
     out = pl.pallas_call(
@@ -421,13 +465,12 @@
         compiler_params=pltpu.CompilerParams(
             collective_id=0, has_side_effects=True, vmem_limit_bytes=62 * 1024 * 1024),
     )(*args)
-    hbm = pl.BlockSpec(memory_space=pltpu.HBM)
+    vmem = pl.BlockSpec(memory_space=pltpu.VMEM)
     return pl.pallas_call(
         functools.partial(deliver, A),
         out_shape=(jax.ShapeDtypeStruct((A, PN, W), F32),) + (jax.ShapeDtypeStruct((PN, W), F32),) * 2,
-        in_specs=[hbm],
-        out_specs=(hbm,) * 3,
-        scratch_shapes=[dma((3,))],
+        in_specs=[vmem],
+        out_specs=(vmem,) * 3,
         compiler_params=pltpu.CompilerParams(vmem_limit_bytes=62 * 1024 * 1024),
     )(out)
 

time: 74.5 us -> 68 us (0.913)
  Pallas kernels: 73.8 us -> 67.3 us
    pallas_call x1, Pallas kernels: 5.1 us -> 1.55 us  [body(): pl.pallas_call(functools.partial(deliver, A), out_shape=(jax.ShapeDtypeSt...]
    pallas_call x1, Pallas kernels: 68.7 us -> 65.7 us  [body(): pl.pallas_call(functools.partial(kernel, S, D, N, B, BPZ, A, K), out_shap...]
where the time goes in v4:
time: 68 us; the launch traced here: 67.9 us
  Pallas kernels  67.3 us (99%)
    pallas_call x1, Pallas kernels, body(): pl.pallas_call(functools.partial(kernel, S, D, N, B, BPZ, A, K), out_shap...  65.7 us
    pallas_call x1, Pallas kernels, body(): pl.pallas_call(functools.partial(deliver, A), out_shape=(jax.ShapeDtypeSt...  1.55 us

profile of v4, /device:TPU:0, one launch (start us, length us, event | category | flops | bytes accessed | tf_op | source)
XLA Modules:
  0.0 67.9 jit_solution(10713759306655492703)
XLA Ops:
  0.6 65.7 %shard_map.112.result = f32[4,16,512]{2,1,0:T(8,128)} custom-call(f32[16,512]{1,0:T(8,128)} %density0_h.1, f32[2,16,512]{2,1,0:T(8,128)} %logits_h.1, f32[16,512]{1,0:T(8,128)} %value_final_h.1, f32[2,16,512]{2,1,0:T(8,128)} %base_reward_h.1, f32[16]{0:T(128)} %crowd_h.1, bf16[4096,256]{1,0:T(8,128)(2,1)} %bitcast.1, s32[1,1,2,8]{3,2,1,0:T(2,128)} %tile_src_h.1, ...), custom_call_target="tpu_custom_call" | custom-call | flops 268435456 | bytes 2097152 | tf_op jit(solution)/shard_map/pallas_call | solution.py:458
  66.3 1.6 %shard_map.113 = (f32[2,16,512]{2,1,0:T(8,128)}, f32[16,512]{1,0:T(8,128)}, f32[16,512]{1,0:T(8,128)}) custom-call(f32[4,16,512]{2,1,0:T(8,128)} %shard_map.112.result), custom_call_target="tpu_custom_call" | custom-call | tf_op jit(solution)/shard_map/pallas_call | solution.py:469

commit v5 on v4

--- a/solution.py
+++ b/solution.py
@@ -152,19 +152,23 @@
                     m = mask[q * DB + c]
                     lhs[c * PN:(c + 1) * PN, q * B:(q + 1) * B] = w * jnp.concatenate([m] * (B // LANES), axis=1)
         arrived = jnp.dot(lhs[...], tiles[...], preferred_element_type=F32)
-        total = arrived[0:PN]
-        for c in range(1, DB):
-            total = total + arrived[c * PN:(c + 1) * PN]
-        packed = pack(total)
         send, recv = (rs_send.at[t], rs_recv.at[t]) if t < 2 else (rz_send.at[t - 2], rz_recv.at[t - 2])
         for c in range(DB):
             part = arrived[c * PN:(c + 1) * PN]
             at = slice((c % BPZ) * B, (c % BPZ + 1) * B)
             arr[c // BPZ, :, at] = part
             send[c // BPZ, :, at] = part.astype(send.dtype)
-        for c in range(S):
-            send[c, :, W:W + LANES] = packed.astype(send.dtype)
-        copies = [start(to_src(send.at[src_peers[r]], recv.at[r - 1], rs_ss.at[t, r - 1], rs_rs.at[t, r - 1], r))
+        if t == 2:
+            packed, width = None, W
+        else:
+            total = arrived[0:PN]
+            for c in range(1, DB):
+                total = total + arrived[c * PN:(c + 1) * PN]
+            packed, width = pack(total), W + LANES
+            for c in range(S):
+                send[c, :, W:W + LANES] = packed.astype(send.dtype)
+        cut = (slice(None), pl.ds(0, width))
+        copies = [start(to_src(send.at[(src_peers[r],) + cut], recv.at[(r - 1,) + cut], rs_ss.at[t, r - 1], rs_rs.at[t, r - 1], r))
                   for r in range(1, S)]
         return copies, recv, packed
 
@@ -174,7 +178,8 @@
         for r in range(1, S):
             copies[r - 1].wait_recv()
             raw = raw + recv[r - 1, :, :W].astype(F32)
-            packed = packed + recv[r - 1, :, W:W + LANES].astype(F32)
+            if packed is not None:
+                packed = packed + recv[r - 1, :, W:W + LANES].astype(F32)
         return raw, packed
 
     def scale_of(packed):

time: 68 us -> 68 us (level)
  no operation moved by 1% of the time
where the time goes in v5:
time: 68 us; the launch traced here: 67.9 us
  Pallas kernels  67.3 us (99%)
    pallas_call x1, Pallas kernels, body(): pl.pallas_call(functools.partial(kernel, S, D, N, B, BPZ, A, K), out_shap...  65.7 us
    pallas_call x1, Pallas kernels, body(): pl.pallas_call(functools.partial(deliver, A), out_shape=(jax.ShapeDtypeSt...  1.55 us

profile of v5, /device:TPU:0, one launch (start us, length us, event | category | flops | bytes accessed | tf_op | source)
XLA Modules:
  0.0 67.9 jit_solution(7823605049161078280)
XLA Ops:
  0.6 65.7 %shard_map.112.result = f32[4,16,512]{2,1,0:T(8,128)} custom-call(f32[16,512]{1,0:T(8,128)} %density0_h.1, f32[2,16,512]{2,1,0:T(8,128)} %logits_h.1, f32[16,512]{1,0:T(8,128)} %value_final_h.1, f32[2,16,512]{2,1,0:T(8,128)} %base_reward_h.1, f32[16]{0:T(128)} %crowd_h.1, bf16[4096,256]{1,0:T(8,128)(2,1)} %bitcast.1, s32[1,1,2,8]{3,2,1,0:T(2,128)} %tile_src_h.1, ...), custom_call_target="tpu_custom_call" | custom-call | flops 268435456 | bytes 2097152 | tf_op jit(solution)/shard_map/pallas_call | solution.py:463
  66.3 1.6 %shard_map.113 = (f32[2,16,512]{2,1,0:T(8,128)}, f32[16,512]{1,0:T(8,128)}, f32[16,512]{1,0:T(8,128)}) custom-call(f32[4,16,512]{2,1,0:T(8,128)} %shard_map.112.result), custom_call_target="tpu_custom_call" | custom-call | tf_op jit(solution)/shard_map/pallas_call | solution.py:474
